TPU v7x, 32 devices: a whole 2x2x4 slice. The times are simulated.
32 devices in a mesh: dom: 4 (over z), grp: 8 (over y, x, core).
Axes of the slice: x: 2, y: 2, z: 4, core: 2. Of those that a mesh axis runs over, the one named last changes fastest.
Arguments:
- src_table: float32 [4096, 400], P(('dom', 'grp')), may hold values from -8 to 8
- src_state: float32 [4096], P(('dom', 'grp')), may hold values from 0.01 to 1
- tgt_table: float32 [32768, 400], P(('dom', 'grp')), may hold values from -8 to 8
- tgt_state: float32 [32768], P(('dom', 'grp')), may hold values from 0.01 to 1
- pair_source: int32 [2, 32768], P(None, ('dom', 'grp')), may hold values from 0 to 127
- pair_owner: int32 [2, 32768, 1], P(None, ('dom', 'grp')), may hold values from 0 to 7; in each aligned block of 1024 rows (0 to 1023, 1024 to 2047, ..., all dimensions but the last counted through in order) at most 256 rows name the same one
- pair_offset: int32 [2, 32768], P(None, ('dom', 'grp')), may hold values from 0 to 1023
- negatives: int32 [4, 1000], P('dom'), may hold values from 0 to 8191
- plan: int32 [2, 4], replicated, may hold values from 0 to 3, each once within a row
Outputs:
- src_trained: float32 [4096, 400], P(('dom', 'grp'))
- src_accum: float32 [4096], P(('dom', 'grp'))
- tgt_trained: float32 [32768, 400], P(('dom', 'grp'))
- tgt_accum: float32 [32768], P(('dom', 'grp'))
Inputs may be any that keep to these rules, and one draw needn't show every extreme that they name: `pair_owner`: in every round the pairs of one device name each owner at most 256 times, and some device's pairs name some owner exactly 256 times. `plan`: each round's row names every dom index once.
All inputs are finite; a program needn't handle non-finite values.
Results may differ from a plain program's by a relative error of at most 0.011.
Values may be sent and summed in bfloat16 or wider, within the bound.
A program may use at most 128 MiB of HBM per device.

v0:
```python
import jax
import jax.numpy as jnp
from jax import lax
from jax.sharding import PartitionSpec as P

LEARN = 0.1


def adagrad(emb_table, opt_state, grads):
    new_state = opt_state + jnp.mean(grads * grads, axis=1)
    return (emb_table - LEARN * grads / jnp.sqrt(new_state)[:, None], new_state)


def slot_holding(sched_row, wanted):
    return jnp.sum(
        jnp.arange(sched_row.shape[0], dtype=jnp.int32) * (sched_row == wanted).astype(jnp.int32)
    )


def relayout(emb_table, opt_state, want_slot):
    carried = (jnp.zeros_like(emb_table), jnp.zeros_like(opt_state))
    pieces = (
        lax.all_gather(emb_table, "dom", axis=0, tiled=True),
        lax.all_gather(opt_state, "dom", axis=0, tiled=True),
    )
    row_count = carried[0].shape[0]
    row_total = pieces[0].shape[0]
    local_index = jnp.arange(row_count, dtype=jnp.int32) + want_slot * row_count
    is_inside = (local_index >= 0) & (local_index < row_total)
    safe_index = jnp.clip(local_index, 0, row_total - 1)
    new_rows = jnp.where(is_inside[:, None], jnp.take(pieces[0], safe_index, axis=0), carried[0])
    new_state = jnp.where(is_inside, jnp.take(pieces[1], safe_index, axis=0), carried[1])
    return (new_rows, new_state)


def train_round(
    held_table, held_state, tgt_table, tgt_state, sources, owners, offsets, neg_ids, my_grp
):
    group_count = lax.axis_size("grp")
    src_count, emb_width = held_table.shape
    tgt_count = tgt_table.shape[0]
    pair_count = sources.shape[0]
    capacity = pair_count // 4
    slot_count = group_count * capacity
    owned_ids = neg_ids - my_grp * tgt_count
    is_mine = (owned_ids >= 0) & (owned_ids < tgt_count)
    owned_safe = jnp.clip(owned_ids, 0, tgt_count - 1)
    src_bf = held_table.astype(jnp.bfloat16)
    tgt_bf = tgt_table.astype(jnp.bfloat16)
    local_rows = jnp.where(is_mine[:, None], jnp.take(tgt_table, owned_safe, axis=0), 0.0)
    neg_rows = lax.psum(local_rows, "grp").astype(jnp.bfloat16)
    dest_onehot = (owners[:, None] == jnp.arange(group_count, dtype=jnp.int32)[None, :]).astype(
        jnp.int32
    )
    slot_rank = jnp.sum((jnp.cumsum(dest_onehot, axis=0) - 1) * dest_onehot, axis=1)
    slot_place = owners * capacity + slot_rank
    out_offsets = jnp.full((slot_count,), -1, jnp.int32).at[slot_place].set(offsets)
    outgoing = (
        jnp.zeros((slot_count, emb_width), jnp.bfloat16)
        .at[slot_place]
        .set(jnp.take(src_bf, sources, axis=0))
    )
    incoming, got_offsets = (
        lax.all_to_all(
            outgoing.reshape(group_count, capacity, emb_width),
            "grp",
            split_axis=0,
            concat_axis=0,
            tiled=True,
        ),
        lax.all_to_all(
            out_offsets.reshape(group_count, capacity),
            "grp",
            split_axis=0,
            concat_axis=0,
            tiled=True,
        ),
    )
    incoming = incoming.reshape(slot_count, emb_width)
    got_offsets = got_offsets.reshape(slot_count)
    is_valid = (got_offsets >= 0).astype(jnp.float32)
    safe_offsets = jnp.clip(got_offsets, 0, tgt_count - 1)
    target_rows = jnp.take(tgt_bf, safe_offsets, axis=0)
    positive = jnp.einsum("sd,sd->s", incoming, target_rows, preferred_element_type=jnp.float32)
    negative = lax.dot_general(
        incoming, neg_rows, (((1,), (1,)), ((), ())), preferred_element_type=jnp.float32
    )
    score_max = jnp.maximum(jnp.max(negative, axis=1), positive)
    pos_exp = jnp.exp(positive - score_max)
    neg_exp = jnp.exp(negative - score_max[:, None])
    exp_total = pos_exp + jnp.sum(neg_exp, axis=1)
    d_pos = (pos_exp / exp_total - 1.0) * is_valid
    d_neg = (neg_exp / exp_total[:, None] * is_valid[:, None]).astype(jnp.bfloat16)
    source_grad = (
        d_pos[:, None] * target_rows.astype(jnp.float32)
        + jnp.dot(d_neg, neg_rows, preferred_element_type=jnp.float32)
    ).astype(jnp.bfloat16)
    returned = lax.all_to_all(
        source_grad.reshape(group_count, capacity, emb_width),
        "grp",
        split_axis=0,
        concat_axis=0,
        tiled=True,
    ).reshape(slot_count, emb_width)
    pair_grad = jnp.take(returned, slot_place, axis=0).astype(jnp.float32)
    src_grads = jnp.zeros((src_count, emb_width), jnp.float32).at[sources].add(pair_grad)
    tgt_grads = (
        jnp.zeros((tgt_count, emb_width), jnp.float32)
        .at[safe_offsets]
        .add(d_pos[:, None] * incoming.astype(jnp.float32))
    )
    neg_part = lax.dot_general(
        d_neg, incoming, (((0,), (0,)), ((), ())), preferred_element_type=jnp.float32
    )
    summed = lax.psum(neg_part, "grp")
    tgt_grads = tgt_grads.at[owned_safe].add(jnp.where(is_mine[:, None], summed, 0.0))
    held_table, held_state = adagrad(held_table, held_state, src_grads)
    tgt_table, tgt_state = adagrad(tgt_table, tgt_state, tgt_grads)
    return (held_table, held_state, tgt_table, tgt_state)


def shards(
    src_table,
    src_state,
    tgt_table,
    tgt_state,
    pair_source,
    pair_owner,
    pair_offset,
    negatives,
    plan,
):
    my_dom = lax.axis_index("dom")
    my_grp = lax.axis_index("grp")
    round_count = plan.shape[0]
    neg_ids = negatives[0]
    for round_index in range(round_count):
        held_table, held_state = relayout(src_table, src_state, plan[round_index, my_dom])
        held_table, held_state, tgt_table, tgt_state = train_round(
            held_table,
            held_state,
            tgt_table,
            tgt_state,
            pair_source[round_index],
            pair_owner[round_index, :, 0],
            pair_offset[round_index],
            neg_ids,
            my_grp,
        )
        src_table, src_state = relayout(
            held_table, held_state, slot_holding(plan[round_index], my_dom)
        )
    return (src_table, src_state, tgt_table, tgt_state)


def solution(mesh):
    return jax.shard_map(
        shards,
        mesh=mesh,
        in_specs=(
            P(("dom", "grp"), None),
            P(("dom", "grp")),
            P(("dom", "grp"), None),
            P(("dom", "grp")),
            P(None, ("dom", "grp")),
            P(None, ("dom", "grp"), None),
            P(None, ("dom", "grp")),
            P("dom", None),
            P(),
        ),
        out_specs=(
            P(("dom", "grp"), None),
            P(("dom", "grp")),
            P(("dom", "grp"), None),
            P(("dom", "grp")),
        ),
        check_vma=False,
    )
```

profile of v0, /device:TPU:0, one launch (start us, length us, event | category | flops | bytes accessed | tf_op | source)
XLA Modules:
  0.0 638.7 jit_solution(1227810447137223901)
XLA Ops:
  39.9 22.7 %all_gather.24 = f32[512,400]{1,0:T(8,128)S(1)} all-gather(f32[128,400]{1,0:T(8,128)S(1)} %copy.65), channel_id=1, replica_groups=mesh['dom'=4,'grp'=8] {'dom'}, dimensions={0}, use_global_device_ids=true | all-gather | bytes 1024000 | tf_op jit(solution)/shard_map/all_gather | solution.py:23
  74.9 54.2 %all-reduce.8 = bf16[1000,400]{0,1:T(8,128)(2,1)} all-reduce(f32[1000,400]{0,1:T(8,128)} %select_select_fusion.1), channel_id=1, replica_groups=mesh['dom'=4,'grp'=8] {'grp'}, use_global_device_ids=true, to_apply=%region_7.12 | all-reduce | flops 400000 | bytes 2400000 | tf_op jit(solution)/shard_map/psum | solution.py:51
  133.3 11.0 %scatter_custom_fusion.1 = bf16[2048,400]{1,0:T(8,128)(2,1)S(1)} fusion(s32[1024]{0:T(1024)S(1)} %bitcast.168, bf16[]{:T(256)} %constant.83.clone.1, pred[1024]{0:T(1024)(128)(4,1)S(1)} %compare_and_fusion.6, bf16[]{:T(256)} %constant.29.clone.2, bf16[128,400]{1,0:T(8,128)(2,1)S(1)} %fusion.38, s32[1024]{0:T(1024)S(1)} %fusion.54), kind=kCustom, calls=%fused_computation.62 | custom fusion | flops 409600 | bytes 1774596 | tf_op jit(solution)/shard_map/scatter | solution.py:61
  147.1 12.5 %all-gather = f32[4,1,128]{2,1,0:T(1,128)S(1)} all-gather(f32[1,1,128]{2,1,0:T(1,128)S(1)} %bitcast.172), channel_id=1, replica_groups=mesh['dom'=4,'grp'=8] {'dom'}, dimensions={0}, use_global_device_ids=true | all-gather | bytes 2560 | tf_op jit(solution)/shard_map/all_gather | solution.py:24
  170.8 7.5 %gather_fusion.1 = bf16[2048,400]{1,0:T(8,128)(2,1)S(1)} fusion(bf16[1024,400]{1,0:T(8,128)(2,1)S(1)} %copy.68, s32[2048]{0:T(1024)S(1)} %fusion.48), kind=kCustom, calls=%fused_computation.2.clone | custom fusion | bytes 3284992 | tf_op jit(solution)/shard_map/jit(_take)/gather | solution.py:83
  189.9 17.3 %all-to-all-done.1 = bf16[8,256,400]{1,2,0:T(8,128)(2,1)S(1)} async-done(((bf16[8,256,400]{1,2,0:T(8,128)(2,1)}), bf16[8,256,400]{1,2,0:T(8,128)(2,1)S(1)}, u32[]{:S(2)}, u32[]{:S(2)}) %all-to-all-start.1) | async-done | bytes 1638432 | tf_op jit(solution)/shard_map/all_to_all | solution.py:64
  237.9 14.9 %scatter_custom_fusion.5 = f32[1024,400]{1,0:T(8,128)S(1)} fusion(s32[2048]{0:T(1024)} %bitcast.161, f32[2048,400]{1,0:T(8,128)} %copy.76, f32[]{:T(128)} %constant.76.clone.1), kind=kCustom, calls=%fused_computation.66 | custom fusion | flops 819200 | bytes 1638912 | tf_op jit(solution)/shard_map/scatter-add | solution.py:110
  252.8 30.6 %all-reduce.5.cloned.1.call-done = f32[1000,400]{0,1:T(8,128)} async-done(((f32[1000,400]{0,1:T(8,128)}), f32[1000,400]{0,1:T(8,128)}) %all-reduce.5.cloned.1.call-update) | async-done | bytes 1600016 | tf_op jit(solution)/shard_map/psum | solution.py:115
  289.1 8.3 %scatter_fusion = f32[1024,400]{1,0:T(8,128)S(1)} fusion(f32[1024,400]{1,0:T(8,128)S(1)} %scatter_custom_fusion.5, s32[1000]{0:T(1024)S(1)} %bitcast.150, f32[1000,400]{1,0:T(8,128)} %copy.77), kind=kCustom, calls=%fused_computation.22 | custom fusion | flops 400000 | bytes 4804000 | tf_op jit(solution)/shard_map/scatter-add | solution.py:116
  301.9 14.4 %scatter_custom_fusion.2 = f32[128,400]{1,0:T(8,128)S(1)} fusion(s32[1024]{0:T(1024)} %bitcast.165, pred[1024]{0:T(1024)(128)(4,1)S(1)} %copy-done.32, bf16[]{:T(256)} %constant.29.clone.2, f32[]{:T(128)} %constant.76.clone.1, bf16[2048,400]{1,0:T(8,128)(2,1)} %bitcast.130, s32[1024]{0:T(1024)S(1)} %copy-done.22), kind=kCustom, calls=%fused_computation.50 | custom fusion | flops 1228800 | bytes 2308096 | tf_op jit(solution)/shard_map/scatter-add | solution.py:106
  317.2 22.9 %all_gather.26 = f32[512,400]{1,0:T(8,128)S(1)} all-gather(f32[128,400]{1,0:T(8,128)S(1)} %divide_subtract_fusion.3), channel_id=1, replica_groups=mesh['dom'=4,'grp'=8] {'dom'}, dimensions={0}, use_global_device_ids=true | all-gather | bytes 1024000 | tf_op jit(solution)/shard_map/all_gather | solution.py:23
  341.1 19.6 %all_gather.27 = f32[512,400]{1,0:T(8,128)S(1)} all-gather(f32[128,400]{1,0:T(8,128)S(1)} %select_select_fusion.4), channel_id=1, replica_groups=mesh['dom'=4,'grp'=8] {'dom'}, dimensions={0}, use_global_device_ids=true | all-gather | bytes 1024000 | tf_op jit(solution)/shard_map/all_gather | solution.py:23
  361.7 12.1 %scatter_custom_fusion.4 = bf16[2048,400]{1,0:T(8,128)(2,1)} fusion(s32[1024]{0:T(1024)} %bitcast.164, bf16[]{:T(256)} %constant.83.clone.1, pred[1024]{0:T(1024)(128)(4,1)S(1)} %copy-done.30, bf16[]{:T(256)} %constant.29.clone.2, bf16[128,400]{1,0:T(8,128)(2,1)S(1)} %fusion.39, s32[1024]{0:T(1024)S(1)} %copy-done.23), kind=kCustom, calls=%fused_computation.59 | custom fusion | flops 409600 | bytes 1746944 | tf_op jit(solution)/shard_map/scatter | solution.py:61
  385.3 5.7 gather_fusion.7
  395.8 7.5 %gather_fusion.6 = bf16[2048,400]{1,0:T(8,128)(2,1)S(1)} fusion(bf16[1024,400]{1,0:T(8,128)(2,1)S(1)} %get-tuple-element.32, s32[2048]{0:T(1024)S(1)} %copy-done.11), kind=kCustom, calls=%fused_computation.10.clone | custom fusion | bytes 3284992 | tf_op jit(solution)/shard_map/jit(_take)/gather | solution.py:83
  405.6 55.0 %all-reduce.9 = bf16[1000,400]{0,1:T(8,128)(2,1)} all-reduce(f32[1000,400]{0,1:T(8,128)} %select_select_fusion), channel_id=1, replica_groups=mesh['dom'=4,'grp'=8] {'grp'}, use_global_device_ids=true, to_apply=%region_21.28 | all-reduce | flops 400000 | bytes 2400000 | tf_op jit(solution)/shard_map/psum | solution.py:51
  460.7 10.0 %all-gather.1 = f32[4,1,128]{2,1,0:T(1,128)S(1)} all-gather(f32[1,1,128]{2,1,0:T(1,128)S(1)} %bitcast.170), channel_id=1, replica_groups=mesh['dom'=4,'grp'=8] {'dom'}, dimensions={0}, use_global_device_ids=true | all-gather | bytes 2560 | tf_op jit(solution)/shard_map/all_gather | solution.py:24
  472.1 7.7 %all-gather.2 = f32[4,1,128]{2,1,0:T(1,128)S(1)} all-gather(f32[1,1,128]{2,1,0:T(1,128)S(1)} %fusion.62), channel_id=1, replica_groups=mesh['dom'=4,'grp'=8] {'dom'}, dimensions={0}, use_global_device_ids=true | all-gather | bytes 2560 | tf_op jit(solution)/shard_map/all_gather | solution.py:24
  513.0 14.8 %scatter_custom_fusion.8 = f32[1024,400]{1,0:T(8,128)S(1)} fusion(s32[2048]{0:T(1024)} %bitcast.160, f32[2048,400]{1,0:T(8,128)} %copy.83, f32[]{:T(128)} %constant.76.clone.1), kind=kCustom, calls=%fused_computation.64 | custom fusion | flops 819200 | bytes 1638912 | tf_op jit(solution)/shard_map/scatter-add | solution.py:110
  527.8 33.1 %all-reduce.7.cloned.1.call-done = f32[1000,400]{0,1:T(8,128)} async-done(((f32[1000,400]{0,1:T(8,128)}), f32[1000,400]{0,1:T(8,128)}) %all-reduce.7.cloned.1.call-update) | async-done | bytes 1600016 | tf_op jit(solution)/shard_map/psum | solution.py:115
  566.5 8.6 %scatter_fusion.1 = f32[1024,400]{1,0:T(8,128)S(1)} fusion(f32[1024,400]{1,0:T(8,128)S(1)} %scatter_custom_fusion.8, s32[1000]{0:T(1024)S(1)} %bitcast.151, f32[1000,400]{1,0:T(8,128)} %copy.84), kind=kCustom, calls=%fused_computation.25 | custom fusion | flops 400000 | bytes 4804000 | tf_op jit(solution)/shard_map/scatter-add | solution.py:116
  584.1 12.1 %scatter_custom_fusion.7 = f32[128,400]{1,0:T(8,128)S(1)} fusion(s32[1024]{0:T(1024)} %bitcast.162, pred[1024]{0:T(1024)(128)(4,1)S(1)} %copy-done.31, bf16[]{:T(256)} %constant.29.clone.2, f32[]{:T(128)} %constant.76.clone.1, bf16[2048,400]{1,0:T(8,128)(2,1)S(1)} %bitcast.129, s32[1024]{0:T(1024)S(1)} %copy-done.21), kind=kCustom, calls=%fused_computation.46 | custom fusion | flops 1228800 | bytes 1849344 | tf_op jit(solution)/shard_map/scatter-add | solution.py:106
  596.6 22.7 %all_gather.30 = f32[512,400]{1,0:T(8,128)S(1)} all-gather(f32[128,400]{1,0:T(8,128)S(1)} %divide_subtract_fusion.2), channel_id=1, replica_groups=mesh['dom'=4,'grp'=8] {'dom'}, dimensions={0}, use_global_device_ids=true | all-gather | bytes 1024000 | tf_op jit(solution)/shard_map/all_gather | solution.py:23
  621.1 8.6 %all-gather.3 = f32[4,1,128]{2,1,0:T(1,128)S(1)} all-gather(f32[1,1,128]{2,1,0:T(1,128)S(1)} %bitcast.171), channel_id=1, replica_groups=mesh['dom'=4,'grp'=8] {'dom'}, dimensions={0}, use_global_device_ids=true | all-gather | bytes 2560 | tf_op jit(solution)/shard_map/all_gather | solution.py:24
  (246 shorter events, 186.8 us)
Async XLA Ops:
  15.0 146.3 %copy-start.33 = (s32[1024,1]{0,1:T(1,128)}, s32[1024,1]{0,1:T(1,128)S(1)}, u32[]{:S(2)}) copy-start(s32[1024,1]{0,1:T(1,128)S(1)} %get-tuple-element.47) | copy-start | bytes 12292
  19.9 146.3 %all-to-all-start = ((s32[8,1,256]{2,1,0:T(1,128)}), s32[8,1,256]{2,1,0:T(1,128)S(1)}, u32[]{:S(2)}, u32[]{:S(2)}) async-start(s32[8,1,256]{2,1,0:T(1,128)} %bitcast.13), calls=%async_computation | async-start | bytes 16384 | tf_op jit(solution)/shard_map/all_to_all | solution.py:71
  30.4 102.0 %copy-start.39 = (pred[128]{0:T(512)(128)(4,1)}, pred[128]{0:T(512)(128)(4,1)S(1)}, u32[]{:S(2)}) copy-start(pred[128]{0:T(512)(128)(4,1)S(1)} %get-tuple-element.58) | copy-start | bytes 388
  30.4 102.0 %copy-start.41 = (pred[128]{0:T(512)(128)(4,1)}, pred[128]{0:T(512)(128)(4,1)S(1)}, u32[]{:S(2)}) copy-start(pred[128]{0:T(512)(128)(4,1)S(1)} %get-tuple-element.59) | copy-start | bytes 388
  31.8 40.3 %copy-start.26 = (pred[1000]{0:T(1024)(128)(4,1)}, pred[1000]{0:T(1024)(128)(4,1)S(1)}, u32[]{:S(2)}) copy-start(pred[1000]{0:T(1024)(128)(4,1)S(1)} %compare_and_fusion.5) | copy-start | bytes 3004
  32.5 39.5 %copy-start.14 = (pred[1000]{0:T(1024)(128)(4,1)}, pred[1000]{0:T(1024)(128)(4,1)S(1)}, u32[]{:S(2)}) copy-start(pred[1000]{0:T(1024)(128)(4,1)S(1)} %and_reduce_fusion) | copy-start | bytes 3004
  74.9 58.2 %copy-start.2 = (f32[1024,400]{0,1:T(8,128)S(1)}, f32[1024,400]{0,1:T(8,128)}, u32[]{:S(2)}) copy-start(f32[1024,400]{0,1:T(8,128)} %param.23) | copy-start | bytes 4915204
  166.3 14.4 %all-to-all-start.3 = ((s32[8,1,256]{2,1,0:T(1,128)}), s32[8,1,256]{2,1,0:T(1,128)S(1)}, u32[]{:S(2)}, u32[]{:S(2)}) async-start(s32[8,1,256]{2,1,0:T(1,128)} %bitcast.30), calls=%async_computation.3 | async-start | bytes 16384 | tf_op jit(solution)/shard_map/all_to_all | solution.py:71
  181.3 25.9 %all-to-all-start.1 = ((bf16[8,256,400]{1,2,0:T(8,128)(2,1)}), bf16[8,256,400]{1,2,0:T(8,128)(2,1)S(1)}, u32[]{:S(2)}, u32[]{:S(2)}) async-start(bf16[8,256,400]{1,2,0:T(8,128)(2,1)} %copy.66), calls=%async_computation.1 | async-start | bytes 3276800 | tf_op jit(solution)/shard_map/all_to_all | solution.py:64
  185.4 98.0 %all-reduce.5.cloned.1.call-start = ((), (), s32[]{:S(2)}) async-start(), calls=%async_computation.6 | async-start | bytes 3276800 | tf_op jit(solution)/shard_map/psum | solution.py:115
  225.7 72.5 %all-to-all-start.2 = ((bf16[8,256,400]{1,2,0:T(8,128)(2,1)}), bf16[8,256,400]{1,2,0:T(8,128)(2,1)}, u32[]{:S(2)}, u32[]{:S(2)}) async-start(bf16[8,256,400]{1,2,0:T(8,128)(2,1)} %bitcast.112), calls=%async_computation.2 | async-start | bytes 3276800 | tf_op jit(solution)/shard_map/all_to_all | solution.py:98
  237.9 45.5 %copy-start.15 = (pred[1000]{0:T(1024)(128)(4,1)S(1)}, pred[1000]{0:T(1024)(128)(4,1)}, u32[]{:S(2)}) copy-start(pred[1000]{0:T(1024)(128)(4,1)} %copy-done.14) | copy-start | bytes 3004
  317.1 23.8 %copy-start.48 = (pred[128]{0:T(512)(128)(4,1)S(1)}, pred[128]{0:T(512)(128)(4,1)}, u32[]{:S(2)}) copy-start(pred[128]{0:T(512)(128)(4,1)} %get-tuple-element.60) | copy-start | bytes 388
  317.1 23.8 %copy-start.49 = (pred[128]{0:T(512)(128)(4,1)S(1)}, pred[128]{0:T(512)(128)(4,1)}, u32[]{:S(2)}) copy-start(pred[128]{0:T(512)(128)(4,1)} %get-tuple-element.61) | copy-start | bytes 388
  341.0 20.5 %copy-start.35 = (pred[128]{0:T(512)(128)(4,1)S(1)}, pred[128]{0:T(512)(128)(4,1)}, u32[]{:S(2)}) copy-start(pred[128]{0:T(512)(128)(4,1)} %get-tuple-element.62) | copy-start | bytes 388
  341.1 20.6 %copy-start.23 = (s32[1024]{0:T(1024)S(1)}, s32[1024]{0:T(1024)}, u32[]{:S(2)}) copy-start(s32[1024]{0:T(1024)} %fusion.55) | copy-start | bytes 12292
  341.1 20.6 %copy-start.30 = (pred[1024]{0:T(1024)(128)(4,1)S(1)}, pred[1024]{0:T(1024)(128)(4,1)}, u32[]{:S(2)}) copy-start(pred[1024]{0:T(1024)(128)(4,1)} %compare_and_fusion.3) | copy-start | bytes 3076
  377.6 104.0 %all-to-all-start.4 = ((bf16[8,256,400]{1,2,0:T(8,128)(2,1)}), bf16[8,256,400]{1,2,0:T(8,128)(2,1)}, u32[]{:S(2)}, u32[]{:S(2)}) async-start(bf16[8,256,400]{1,2,0:T(8,128)(2,1)} %copy.74), calls=%async_computation.4 | async-start | bytes 3276800 | tf_op jit(solution)/shard_map/all_to_all | solution.py:64
  381.9 179.0 %all-reduce.7.cloned.1.call-start = ((), (), s32[]{:S(2)}) async-start(), calls=%async_computation.7 | async-start | bytes 3276800 | tf_op jit(solution)/shard_map/psum | solution.py:115
  405.6 55.0 %copy-start.34 = (f32[128]{0:T(128)S(1)}, f32[128]{0:T(128)}, u32[]{:S(2)}) copy-start(f32[128]{0:T(128)} %get-tuple-element.37) | copy-start | bytes 1540
  501.3 79.9 %all-to-all-start.5 = ((bf16[8,256,400]{1,2,0:T(8,128)(2,1)}), bf16[8,256,400]{1,2,0:T(8,128)(2,1)}, u32[]{:S(2)}, u32[]{:S(2)}) async-start(bf16[8,256,400]{1,2,0:T(8,128)(2,1)} %bitcast.111), calls=%async_computation.5 | async-start | bytes 3276800 | tf_op jit(solution)/shard_map/all_to_all | solution.py:98
  513.0 47.9 %copy-start.16 = (pred[1000]{0:T(1024)(128)(4,1)S(1)}, pred[1000]{0:T(1024)(128)(4,1)}, u32[]{:S(2)}) copy-start(pred[1000]{0:T(1024)(128)(4,1)} %copy-done.14) | copy-start | bytes 3004
  596.4 23.8 %copy-start.46 = (pred[128]{0:T(512)(128)(4,1)S(1)}, pred[128]{0:T(512)(128)(4,1)}, u32[]{:S(2)}) copy-start(pred[128]{0:T(512)(128)(4,1)} %get-tuple-element.64) | copy-start | bytes 388
  596.4 23.8 %copy-start.47 = (pred[128]{0:T(512)(128)(4,1)S(1)}, pred[128]{0:T(512)(128)(4,1)}, u32[]{:S(2)}) copy-start(pred[128]{0:T(512)(128)(4,1)} %get-tuple-element.65) | copy-start | bytes 388
  (34 other events, 174.8 us)
Sparse Core Ops, SparseCore 0:
  219.7 63.6 all-reduce.4
  495.6 65.2 all-reduce.6
where the time goes:
time: 649 us; the launch traced here: 639 us
  blocking collectives  236 us (36%)
  other arithmetic  150 us (23%)
  local copies, waits for them, and re-layouts  105 us (16%)
  waiting for transfers between devices  81 us (12%)
  starting transfers between devices  26 us (4%)
  matrix products  22.8 us (4%)
  between operations  18 us (3%)
    psum x2, blocking collectives, train_round(): neg_rows = lax.psum(local_rows, 'grp').astype(jnp.bfloat16)  109 us
    all_gather x4, blocking collectives, relayout(): lax.all_gather(emb_table, 'dom', axis=0, tiled=True)  87.8 us
    psum x2, waiting for transfers between devices, train_round(): summed = lax.psum(neg_part, 'grp')  63.7 us
    all_gather x4, blocking collectives, relayout(): lax.all_gather(opt_state, 'dom', axis=0, tiled=True)  38.7 us
    scatter-add x2, other arithmetic, train_round(): tgt_grads = jnp.zeros((tgt_count, emb_width), jnp.float32).at[safe_offset...  29.7 us
    scatter-add x2, other arithmetic, train_round(): jnp.zeros((src_count, emb_width), jnp.float32).at[sources].add(pair_grad)  26.6 us
    scatter x2, other arithmetic, train_round(): outgoing = jnp.zeros((slot_count, emb_width), jnp.bfloat16).at[slot_place...  23.1 us
    gather x4, local copies, waits for them, and re-layouts, train_round(): target_rows = jnp.take(tgt_bf, safe_offsets, axis=0)  19.7 us
  transfers between devices with their start and end apart: 8, of which 3 were waited for; matrix products, arithmetic and copies ran while one was open for 28% of the time, Pallas kernels for 0%

commit v1 on v0

v1 whole, which is shorter than its diff:
```python
import functools

import jax
import jax.numpy as jnp
from jax import lax
from jax.experimental import pallas as pl
from jax.experimental.pallas import tpu as pltpu
from jax.sharding import PartitionSpec as P

LEARN = 0.1
LOW = -1e30
ROWS, STATS, SUMS, BACK, HOME, NAMES, GROUP = range(7)
NT = (((1,), (1,)), ((), ()))
TN = (((0,), (0,)), ((), ()))


def train_kernel(
    n_dom,
    n_grp,
    rounds,
    plan,
    negs,
    names,
    src_in,
    src_state_in,
    tgt_in,
    tgt_state_in,
    src,
    src_state,
    tgt,
    tgt_state,
    name_all,
    mult,
    tgt_bf,
    row_all,
    src_all,
    scores,
    pulls,
    counts,
    weights,
    stat_all,
    sum_all,
    back_out,
    back_all,
    home_all,
    send_sem,
    recv_sem,
):
    my_dom = lax.axis_index("dom")
    my_grp = lax.axis_index("grp")
    src_dev, width = src.shape
    tgt_dev = tgt.shape[0]
    tile = 256
    tiles = tgt_dev // tile
    src_part = n_grp * src_dev
    f32, bf16 = jnp.float32, jnp.bfloat16

    def peers(axis, body):
        size, me = (n_dom, my_dom) if axis == "dom" else (n_grp, my_grp)

        @pl.loop(1, size)
        def _(step):
            body(step, lax.rem(me + step, size))

    def copy(kind, r, axis, step, peer, source, target):
        return pltpu.make_async_remote_copy(
            src_ref=source,
            dst_ref=target,
            send_sem=send_sem.at[r, kind, step],
            recv_sem=recv_sem.at[r, kind, step],
            device_id={axis: peer},
            device_id_type=pl.DeviceIdType.MESH,
        )

    def spread(kind, r, axis, source, target):
        peers(axis, lambda step, peer: copy(kind, r, axis, step, peer, source, target).start())

    def gathered(kind, r, axis, source, target):
        peers(axis, lambda step, peer: copy(kind, r, axis, step, peer, source, target).wait())

    def rows_of(index):
        return pl.ds(pl.multiple_of(index * tile, tile), tile)

    def count_pairs(r):
        @pl.loop(0, n_grp)
        def _(g):
            source = name_all[g, r, 0:1, :]
            target = name_all[g, r, 1:2, :] - my_grp * tgt_dev
            pairs = source.shape[1]
            source_hot = jnp.where(
                lax.broadcasted_iota(jnp.int32, (src_dev, pairs), 0) == source, 1.0, 0.0
            ).astype(bf16)
            columns = pl.ds(pl.multiple_of(g * src_dev, src_dev), src_dev)

            @pl.loop(0, tiles)
            def _(i):
                target_hot = jnp.where(
                    lax.broadcasted_iota(jnp.int32, (tile, pairs), 0) == target - i * tile, 1.0, 0.0
                ).astype(bf16)
                counts[rows_of(i), columns] = lax.dot_general(
                    target_hot, source_hot, NT, preferred_element_type=f32
                ).astype(bf16)

    barrier = pltpu.get_barrier_semaphore()

    def greet(axis):
        def body(step, peer):
            pl.semaphore_signal(
                barrier, inc=1, device_id={axis: peer}, device_id_type=pl.DeviceIdType.MESH
            )

        peers(axis, body)

    greet("dom")
    greet("grp")
    row_all[0, my_dom] = src_in[...].astype(bf16)
    name_all[my_grp] = names[...]
    pl.semaphore_wait(barrier, n_dom + n_grp - 2)
    spread(NAMES, 0, "grp", name_all.at[my_grp], name_all.at[my_grp])
    spread(ROWS, 0, "dom", row_all.at[0, my_dom], row_all.at[0, my_dom])

    src[...] = src_in[...]
    src_state[...] = src_state_in[...]

    @pl.loop(0, tiles)
    def _(i):
        here = lax.broadcasted_iota(jnp.int32, (tile, negs.shape[1]), 0)
        wanted = negs[...] - (my_grp * tgt_dev + i * tile)
        mult[rows_of(i)] = jnp.sum(jnp.where(here == wanted, 1.0, 0.0), axis=1, keepdims=True)
        tgt[rows_of(i)] = tgt_in[rows_of(i)]
        tgt_bf[rows_of(i)] = tgt_in[rows_of(i)].astype(bf16)
        tgt_state[rows_of(i)] = tgt_state_in[rows_of(i)]

    gathered(NAMES, 0, "grp", name_all.at[my_grp], name_all.at[my_grp])
    count_pairs(0)

    @pl.loop(0, rounds)
    def _(r):
        gathered(ROWS, r, "dom", row_all.at[r, my_dom], row_all.at[r, my_dom])
        src_all[r, my_grp] = row_all[r, plan[r, my_dom]]
        mine = src_all.at[r, my_grp]
        spread(GROUP, r, "grp", mine, mine)
        gathered(GROUP, r, "grp", mine, mine)
        sources = src_all[r].reshape(src_part, width)

        def score(i, top):
            found = lax.dot_general(tgt_bf[rows_of(i)], sources, NT, preferred_element_type=f32)
            scores[rows_of(i)] = found
            named = jnp.where(mult[rows_of(i)] > 0, found, LOW)
            return jnp.maximum(top, jnp.max(named, axis=0, keepdims=True))

        top = lax.fori_loop(0, tiles, score, jnp.full((1, src_part), LOW, f32))

        def add_exp(i, total):
            many = mult[rows_of(i)]
            named = jnp.where(many > 0, scores[rows_of(i)], LOW)
            return total + jnp.sum(many * jnp.exp(named - top), axis=0, keepdims=True)

        total = lax.fori_loop(0, tiles, add_exp, jnp.zeros((1, src_part), f32))
        stat_all[r, my_grp, 0:1, :] = top
        stat_all[r, my_grp, 1:2, :] = total
        mine = stat_all.at[r, my_grp]
        spread(STATS, r, "grp", mine, mine)
        gathered(STATS, r, "grp", mine, mine)
        top = stat_all[r, 0, 0:1, :]
        for g in range(1, n_grp):
            top = jnp.maximum(top, stat_all[r, g, 0:1, :])
        total = jnp.zeros((1, src_part), f32)
        for g in range(n_grp):
            total += stat_all[r, g, 1:2, :] * jnp.exp(stat_all[r, g, 0:1, :] - top)
        log_total = jnp.log(total)
        part = 1.0 / total

        def pull(i, pulled):
            many = mult[rows_of(i)]
            found = scores[rows_of(i)]
            gap = (top - found) + log_total
            small = jnp.exp(-jnp.abs(gap))
            miss = jnp.where(gap >= 0, 1.0, small) / (1.0 + small)
            miss = miss * counts[rows_of(i)].astype(f32)
            pulls[rows_of(i)] = miss
            scores[rows_of(i)] = many * jnp.exp(jnp.where(many > 0, found, LOW) - top) * part
            return pulled + jnp.sum(miss, axis=0, keepdims=True)

        pulled = lax.fori_loop(0, tiles, pull, jnp.zeros((1, src_part), f32))
        sum_all[r, my_grp] = pulled
        mine = sum_all.at[r, my_grp]
        spread(SUMS, r, "grp", mine, mine)
        gathered(SUMS, r, "grp", mine, mine)
        pulled = sum_all[r, 0]
        for g in range(1, n_grp):
            pulled += sum_all[r, g]

        @pl.loop(0, tiles)
        def _(i):
            weights[rows_of(i)] = (pulled * scores[rows_of(i)] - pulls[rows_of(i)]).astype(bf16)

        both = 2 * src_dev
        pairs_of = n_grp // 2

        @pl.loop(0, pairs_of)
        def _(step):
            chip = lax.rem(my_grp // 2 + step, pairs_of)
            columns = pl.ds(pl.multiple_of(chip * both, both), both)
            grads = lax.dot_general(
                weights[:, columns], tgt_bf[...], TN, preferred_element_type=f32
            ).astype(bf16)
            for core in range(2):
                peer = chip * 2 + core
                back_out[r, peer] = grads[core * src_dev : (core + 1) * src_dev]

                @pl.when(peer != my_grp)
                def _():
                    copy(
                        BACK,
                        r,
                        "grp",
                        lax.rem(peer - my_grp + n_grp, n_grp),
                        peer,
                        back_out.at[r, peer],
                        back_all.at[r, my_grp],
                    ).start()

        @pl.loop(0, tiles)
        def _(i):
            grads = jnp.dot(weights[rows_of(i)], sources, preferred_element_type=f32)
            state = tgt_state[rows_of(i)] + jnp.sum(grads * grads, axis=1, keepdims=True) / width
            tgt_state[rows_of(i)] = state
            rows = tgt[rows_of(i)] - (LEARN * grads) / jnp.sqrt(state)
            tgt[rows_of(i)] = rows
            tgt_bf[rows_of(i)] = rows.astype(bf16)

        @pl.when(r + 1 < rounds)
        def _():
            count_pairs(r + 1)

        back_all[r, my_grp] = back_out[r, my_grp]
        peers(
            "grp",
            lambda step, peer: copy(
                BACK, r, "grp", step, peer, back_out.at[r, peer], back_all.at[r, my_grp]
            ).wait(),
        )
        grads = back_all[r, 0].astype(f32)
        for g in range(1, n_grp):
            grads += back_all[r, g].astype(f32)
        home_all[r, my_dom] = grads.astype(bf16)
        mine = home_all.at[r, my_dom]
        spread(HOME, r, "dom", mine, mine)
        gathered(HOME, r, "dom", mine, mine)
        trainer = jnp.int32(0)
        for d in range(n_dom):
            trainer = jnp.where(plan[r, d] == my_dom, d, trainer)
        grads = home_all[r, trainer].astype(f32)
        state = src_state[...] + jnp.sum(grads * grads, axis=1, keepdims=True) / width
        src_state[...] = state
        rows = src[...] - (LEARN * grads) / jnp.sqrt(state)
        src[...] = rows

        @pl.when(r + 1 < rounds)
        def _():
            row_all[r + 1, my_dom] = rows.astype(bf16)
            mine = row_all.at[r + 1, my_dom]
            spread(ROWS, r + 1, "dom", mine, mine)


def shards(
    n_dom,
    n_grp,
    src_table,
    src_state,
    tgt_table,
    tgt_state,
    pair_source,
    pair_owner,
    pair_offset,
    negatives,
    plan,
):
    rounds = plan.shape[0]
    src_dev, width = src_table.shape
    tgt_dev = tgt_table.shape[0]
    src_part = n_grp * src_dev
    f32, bf16 = jnp.float32, jnp.bfloat16
    names = jnp.stack([pair_source, pair_owner[:, :, 0] * tgt_dev + pair_offset], axis=1)
    vmem = pl.BlockSpec(memory_space=pltpu.VMEM)
    steps = max(n_dom, n_grp)
    new_src, new_src_state, new_tgt, new_tgt_state = pl.pallas_call(
        functools.partial(train_kernel, n_dom, n_grp, rounds),
        out_shape=(
            jax.ShapeDtypeStruct((src_dev, width), f32),
            jax.ShapeDtypeStruct((src_dev, 1), f32),
            jax.ShapeDtypeStruct((tgt_dev, width), f32),
            jax.ShapeDtypeStruct((tgt_dev, 1), f32),
        ),
        in_specs=[pl.BlockSpec(memory_space=pltpu.SMEM)] + [vmem] * 6,
        out_specs=[vmem] * 4,
        scratch_shapes=[
            pltpu.VMEM((n_grp,) + names.shape, jnp.int32),
            pltpu.VMEM((tgt_dev, 1), f32),
            pltpu.VMEM((tgt_dev, width), bf16),
            pltpu.VMEM((rounds, n_dom, src_dev, width), bf16),
            pltpu.VMEM((rounds, n_grp, src_dev, width), bf16),
            pltpu.VMEM((tgt_dev, src_part), f32),
            pltpu.VMEM((tgt_dev, src_part), f32),
            pltpu.VMEM((tgt_dev, src_part), bf16),
            pltpu.VMEM((tgt_dev, src_part), bf16),
            pltpu.VMEM((rounds, n_grp, 2, src_part), f32),
            pltpu.VMEM((rounds, n_grp, 1, src_part), f32),
            pltpu.VMEM((rounds, n_grp, src_dev, width), bf16),
            pltpu.VMEM((rounds, n_grp, src_dev, width), bf16),
            pltpu.VMEM((rounds, n_dom, src_dev, width), bf16),
            pltpu.SemaphoreType.DMA((rounds, 7, steps)),
            pltpu.SemaphoreType.DMA((rounds, 7, steps)),
        ],
        compiler_params=pltpu.CompilerParams(
            collective_id=0, has_side_effects=True, vmem_limit_bytes=56 * 1024 * 1024
        ),
        name="train",
    )(
        plan,
        negatives,
        names,
        src_table,
        src_state[:, None],
        tgt_table,
        tgt_state[:, None],
    )
    return (new_src, new_src_state[:, 0], new_tgt, new_tgt_state[:, 0])


def solution(mesh):
    return jax.shard_map(
        functools.partial(shards, mesh.shape["dom"], mesh.shape["grp"]),
        mesh=mesh,
        in_specs=(
            P(("dom", "grp"), None),
            P(("dom", "grp")),
            P(("dom", "grp"), None),
            P(("dom", "grp")),
            P(None, ("dom", "grp")),
            P(None, ("dom", "grp"), None),
            P(None, ("dom", "grp")),
            P("dom", None),
            P(),
        ),
        out_specs=(
            P(("dom", "grp"), None),
            P(("dom", "grp")),
            P(("dom", "grp"), None),
            P(("dom", "grp")),
        ),
        check_vma=False,
    )
```

time: 649 us -> 157 us (0.24); the launches traced: 639 us -> 156 us
  blocking collectives: 236 us -> 0 us
  other arithmetic: 150 us -> 4.64 us
  Pallas kernels: 0 us -> 138 us
  local copies, waits for them, and re-layouts: 105 us -> 12.9 us
  waiting for transfers between devices: 81 us -> 0 us
  starting transfers between devices: 26 us -> 0 us
  matrix products: 22.8 us -> 0 us
  between operations: 18 us -> 0.65 us
    pallas_call x0 -> x1, Pallas kernels: none -> 138 us  [shards(): pl.pallas_call(functools.partial(train_kernel, n_dom, n_grp, rounds), out...]
    all_gather x8 -> x0, blocking collectives: 127 us -> none  [the longest x4 87.8 us: relayout(): lax.all_gather(emb_table, 'dom', axis=0, tiled=True)]
    psum x2 -> x0, blocking collectives: 109 us -> none  [train_round(): neg_rows = lax.psum(local_rows, 'grp').astype(jnp.bfloat16)]
    scatter-add x6 -> x0, other arithmetic: 73.2 us -> none  [the longest x2 29.7 us: train_round(): tgt_grads = jnp.zeros((tgt_count, emb_width), jnp.float32).at[safe_offset...]
    psum x2 -> x0, waiting for transfers between devices: 63.7 us -> none  [train_round(): summed = lax.psum(neg_part, 'grp')]
    gather x16 -> x0, local copies, waits for them, and re-layouts: 44.6 us -> none  [the longest x4 19.7 us: train_round(): target_rows = jnp.take(tgt_bf, safe_offsets, axis=0)]
    all_to_all x6 -> x0, starting transfers between devices: 26 us -> none  [the longest x2 9.05 us: train_round(): lax.all_to_all(source_grad.reshape(group_count, capacity, emb_width), 'gr...]
    scatter x2 -> x0, other arithmetic: 23.1 us -> none  [train_round(): outgoing = jnp.zeros((slot_count, emb_width), jnp.bfloat16).at[slot_place...]
  transfers between devices with their start and end apart: 8 -> 0, of which waited for: 3 -> 0; matrix products, arithmetic and copies ran while one was open for 28% -> 0% of each run, Pallas kernels for 0% -> 0%
where the time goes in v1:
time: 157 us; the launch traced here: 156 us
  Pallas kernels  138 us (88%)
  local copies, waits for them, and re-layouts  12.9 us (8%)
  other arithmetic  4.64 us (3%)
    pallas_call x1, Pallas kernels, shards(): pl.pallas_call(functools.partial(train_kernel, n_dom, n_grp, rounds), out...  138 us
    unnamed x4, local copies, waits for them, and re-layouts  9.14 us
    pallas_call x2, other arithmetic, shards(): pl.pallas_call(functools.partial(train_kernel, n_dom, n_grp, rounds), out...  3.31 us

profile of v1, /device:TPU:0, one launch (start us, length us, event | category | flops | bytes accessed | tf_op | source)
XLA Modules:
  0.0 156.4 jit_solution(15244455579976464661)
XLA Ops:
  0.6 0.7 stack.9
  1.3 0.7 bitcast_add_fusion
  2.1 0.6 pad_add_fusion.names
  2.7 1.4 copy.21.src_state_in
  4.1 1.8 %copy.20.src_in = f32[128,400]{1,0:T(8,128)} copy(f32[128,400]{0,1:T(8,128)} %param.9) | data formatting | bytes 409600 | tf_op args[0]
  5.8 1.7 %copy.23.tgt_state_in = f32[1024,1]{1,0:T(8,128)} copy(f32[1024,1]{0,1:T(1,128)} %bitcast.4) | data formatting | bytes 8192 | tf_op jit(solution)/shard_map/broadcast_in_dim | solution.py:327
  7.5 2.9 %copy.22.tgt_in = f32[1024,400]{1,0:T(8,128)} copy(f32[1024,400]{0,1:T(8,128)} %param.11) | data formatting | bytes 3276800 | tf_op args[2]
  10.4 138.1 %train.1 = (f32[128,400]{1,0:T(8,128)}, f32[128,1]{1,0:T(8,128)}, f32[1024,400]{1,0:T(8,128)}, f32[1024,1]{1,0:T(8,128)}) custom-call(s32[2,4]{1,0:T(2,128)} %plan.1, s32[1,1000]{1,0:T(1,128)} %negs.1, s32[2,2,1024]{2,1,0:T(2,128)} %pad_add_fusion.names, f32[128,400]{1,0:T(8,128)} %copy.20.src_in, f32[128,1]{1,0:T(8,128)} %copy.21.src_state_in, ...), custom_call_target="tpu_custom_call" | custom-call | tf_op jit(solution)/shard_map/train/pallas_call | solution.py:288
  148.6 1.8 %copy.24 = f32[128,400]{0,1:T(8,128)} copy(f32[128,400]{1,0:T(8,128)} %get-tuple-element.16) | data formatting | bytes 409600
  150.3 1.5 reduce
  151.8 1.8 %reduce.1 = f32[1024]{0:T(1024)} reduce(f32[1024,1]{1,0:T(8,128)} %get-tuple-element.11, f32[]{:T(128)} %constant.3), dimensions={1}, to_apply=%get-tuple-element.11.reduce_sub_computation | reduce | bytes 8196 | tf_op jit(solution)/shard_map/train/pallas_call | solution.py:288
  153.6 2.7 %copy.25 = f32[1024,400]{0,1:T(8,128)} copy(f32[1024,400]{1,0:T(8,128)} %get-tuple-element.18) | data formatting | bytes 3276800
  (1 shorter events, 0.0 us)

commit v2 on v1

v2 whole, which is shorter than its diff:
```python
import functools

import jax
import jax.numpy as jnp
from jax import lax
from jax.experimental import pallas as pl
from jax.experimental.pallas import tpu as pltpu
from jax.sharding import PartitionSpec as P

LEARN = 0.1
LOW = -1e30
ROWS, STATS, SUMS, BACK, HOME, NAMES, GROUP, PASS, PART, FULL, STATE, KINDS = range(12)
NT = (((1,), (1,)), ((), ()))


def train_kernel(
    n_dom,
    n_grp,
    rounds,
    plan,
    negs,
    pair_source,
    pair_owner,
    pair_offset,
    src_in,
    src_state_in,
    tgt_in,
    tgt_state_in,
    src,
    src_state,
    tgt,
    tgt_state,
    name_all,
    mult,
    tgt_bf,
    tgt_rows,
    row_all,
    full_all,
    state_all,
    src_all,
    scores,
    pulls,
    counts,
    weights,
    stat_all,
    sum_all,
    part_own,
    part_got,
    back_out,
    back_all,
    home_all,
    send_sem,
    recv_sem,
):
    my_dom = lax.axis_index("dom")
    my_grp = lax.axis_index("grp")
    chips = n_grp // 2
    my_chip, my_core = my_grp // 2, lax.rem(my_grp, 2)
    sibling = my_chip * 2 + 1 - my_core
    width, src_dev = src.shape
    tgt_dev = tgt.shape[1]
    tile = 256
    tiles = tgt_dev // tile
    both = 2 * src_dev
    src_part = n_grp * src_dev
    f32, bf16 = jnp.float32, jnp.bfloat16

    def peers(axis, body):
        size, me = (n_dom, my_dom) if axis == "dom" else (n_grp, my_grp)

        @pl.loop(1, size)
        def _(step):
            body(step, lax.rem(me + step, size))

    def copy(kind, r, axis, step, peer, source, target):
        return pltpu.make_async_remote_copy(
            src_ref=source,
            dst_ref=target,
            send_sem=send_sem.at[r, kind, step],
            recv_sem=recv_sem.at[r, kind, step],
            device_id={axis: peer},
            device_id_type=pl.DeviceIdType.MESH,
        )

    def spread(kind, r, axis, ref):
        peers(axis, lambda step, peer: copy(kind, r, axis, step, peer, ref, ref).start())

    def gathered(kind, r, axis, ref):
        peers(axis, lambda step, peer: copy(kind, r, axis, step, peer, ref, ref).wait())

    def span(index, size):
        return pl.ds(pl.multiple_of(index * size, size), size)

    def rows_of(index):
        return span(index, tile)

    def count_pairs(r, first, last):
        @pl.loop(first, last)
        def _(g):
            source = name_all[g, 0, pl.ds(r, 1), :]
            target = name_all[g, 1, pl.ds(r, 1), :] - my_grp * tgt_dev
            pairs = source.shape[1]
            source_hot = jnp.where(
                lax.broadcasted_iota(jnp.int32, (src_dev, pairs), 0) == source, 1.0, 0.0
            ).astype(bf16)

            @pl.loop(0, tiles)
            def _(i):
                target_hot = jnp.where(
                    lax.broadcasted_iota(jnp.int32, (tile, pairs), 0) == target - i * tile, 1.0, 0.0
                ).astype(bf16)
                counts[rows_of(i), span(g, src_dev)] = lax.dot_general(
                    target_hot, source_hot, NT, preferred_element_type=f32
                ).astype(bf16)

    barrier = pltpu.get_barrier_semaphore()

    def greet(axis):
        def body(step, peer):
            pl.semaphore_signal(
                barrier, inc=1, device_id={axis: peer}, device_id_type=pl.DeviceIdType.MESH
            )

        peers(axis, body)

    greet("dom")
    greet("grp")
    row_all[my_dom] = src_in[...].astype(bf16)
    full_all[my_dom] = src_in[...]
    state_all[my_dom] = src_state_in[...]
    name_all[my_grp, 0] = pair_source[...]
    name_all[my_grp, 1] = pair_owner[...] * tgt_dev + pair_offset[...]
    pl.semaphore_wait(barrier, n_dom + n_grp - 2)
    spread(ROWS, 0, "dom", row_all.at[my_dom])
    spread(NAMES, 0, "grp", name_all.at[my_grp])

    @pl.loop(0, tiles)
    def _(i):
        here = lax.broadcasted_iota(jnp.int32, (tile, negs.shape[1]), 0)
        wanted = negs[...] - (my_grp * tgt_dev + i * tile)
        mult[rows_of(i)] = jnp.sum(jnp.where(here == wanted, 1.0, 0.0), axis=1, keepdims=True)
        rows = tgt_in[:, rows_of(i)]
        tgt[:, rows_of(i)] = rows
        tgt_bf[:, rows_of(i)] = rows.astype(bf16)
        tgt_rows[rows_of(i)] = rows.T.astype(bf16)

    tgt_state[...] = tgt_state_in[...]
    gathered(NAMES, 0, "grp", name_all.at[my_grp])
    count_pairs(0, 0, chips)
    gathered(ROWS, 0, "dom", row_all.at[my_dom])
    src_all[0, :, span(my_grp, src_dev)] = row_all[plan[0, my_dom]]

    @pl.loop(0, rounds)
    def _(r):
        def column(index):
            return src_all.at[r, :, span(index, src_dev)]

        def to_chip(step):
            peer = lax.rem(my_chip + step, chips) * 2 + my_core
            return copy(GROUP, r, "grp", step, peer, column(my_grp), column(my_grp))

        def to_sibling(step):
            held = lax.rem(my_chip - step + chips, chips) * 2 + my_core
            return copy(PASS, r, "grp", step, sibling, column(held), column(held))

        for step in range(1, chips):
            to_chip(step).start()
        to_sibling(0).start()

        @pl.when(r == 0)
        def _():
            spread(FULL, 0, "dom", full_all.at[my_dom])
            spread(STATE, 0, "dom", state_all.at[my_dom])

        count_pairs(r, chips, n_grp)

        def score_chip(chip):
            columns = span(chip, both)

            def score(i, top):
                found = jnp.dot(
                    tgt_rows[rows_of(i)], src_all[r, :, columns], preferred_element_type=f32
                )
                scores[rows_of(i), columns] = found
                named = jnp.where(mult[rows_of(i)] > 0, found, LOW)
                return jnp.maximum(top, jnp.max(named, axis=0, keepdims=True))

            top = lax.fori_loop(0, tiles, score, jnp.full((1, both), LOW, f32))

            def add_exp(i, total):
                many = mult[rows_of(i)]
                named = jnp.where(many > 0, scores[rows_of(i), columns], LOW)
                return total + jnp.sum(many * jnp.exp(named - top), axis=0, keepdims=True)

            total = lax.fori_loop(0, tiles, add_exp, jnp.zeros((1, both), f32))
            stat_all[r, my_grp, 0:1, columns] = top
            stat_all[r, my_grp, 1:2, columns] = total

        for step in range(1, chips + 1):
            if step < chips:
                to_chip(step).wait()
                to_sibling(step).start()
            to_sibling(step - 1).wait()
            score_chip(lax.rem(my_chip - (step - 1) + chips, chips))

        spread(STATS, r, "grp", stat_all.at[r, my_grp])
        gathered(STATS, r, "grp", stat_all.at[r, my_grp])
        top = stat_all[r, 0, 0:1, :]
        for g in range(1, n_grp):
            top = jnp.maximum(top, stat_all[r, g, 0:1, :])
        total = jnp.zeros((1, src_part), f32)
        for g in range(n_grp):
            total += stat_all[r, g, 1:2, :] * jnp.exp(stat_all[r, g, 0:1, :] - top)
        log_total = jnp.log(total)
        part = 1.0 / total

        def pull(i, pulled):
            found = scores[rows_of(i)]
            gap = (top - found) + log_total
            small = jnp.exp(-jnp.abs(gap))
            miss = jnp.where(gap >= 0, 1.0, small) / (1.0 + small)
            miss = miss * counts[rows_of(i)].astype(f32)
            pulls[rows_of(i)] = miss
            return pulled + jnp.sum(miss, axis=0, keepdims=True)

        pulled = lax.fori_loop(0, tiles, pull, jnp.zeros((1, src_part), f32))
        sum_all[r, my_grp] = pulled
        spread(SUMS, r, "grp", sum_all.at[r, my_grp])

        @pl.loop(0, tiles)
        def _(i):
            many = mult[rows_of(i)]
            named = jnp.where(many > 0, scores[rows_of(i)], LOW)
            scores[rows_of(i)] = many * jnp.exp(named - top) * part

        gathered(SUMS, r, "grp", sum_all.at[r, my_grp])
        pulled = sum_all[r, 0]
        for g in range(1, n_grp):
            pulled += sum_all[r, g]

        @pl.loop(0, tiles)
        def _(i):
            weights[rows_of(i)] = (pulled * scores[rows_of(i)] - pulls[rows_of(i)]).astype(bf16)

        mine, other = span(my_core, src_dev), span(1 - my_core, src_dev)

        def give_part(step):
            return copy(
                PART, r, "grp", step, sibling, part_own.at[r, step, :, other], part_got.at[r, step]
            )

        def give_back(step):
            peer = lax.rem(my_chip + step, chips) * 2 + my_core
            return copy(BACK, r, "grp", step, peer, back_out.at[r, step], back_all.at[r, step])

        def chip_sum(step):
            give_part(step).wait()
            return part_own[r, step, :, mine].astype(f32) + part_got[r, step].astype(f32)

        for turn in range(1, chips + 1):
            step = turn % chips
            columns = span(lax.rem(my_chip + step, chips), both)
            part_own[r, step] = jnp.dot(
                tgt_bf[...], weights[:, columns], preferred_element_type=f32
            ).astype(bf16)
            give_part(step).start()
            if turn > 1:
                back_out[r, turn - 1] = chip_sum(turn - 1).astype(bf16)
                give_back(turn - 1).start()

        @pl.loop(0, tiles)
        def _(i):
            grads = lax.dot_general(
                src_all[r], weights[rows_of(i)], NT, preferred_element_type=f32
            )
            state = tgt_state[:, rows_of(i)] + jnp.sum(grads * grads, axis=0, keepdims=True) / width
            tgt_state[:, rows_of(i)] = state
            rows = tgt[:, rows_of(i)] - (LEARN * grads) / jnp.sqrt(state)
            tgt[:, rows_of(i)] = rows

            @pl.when(r + 1 < rounds)
            def _():
                tgt_bf[:, rows_of(i)] = rows.astype(bf16)
                tgt_rows[rows_of(i)] = rows.T.astype(bf16)

        grads = chip_sum(0)
        for step in range(1, chips):
            give_back(step).wait()
            grads += back_all[r, step].astype(f32)
        home_all[r, my_dom] = grads.astype(bf16)
        spread(HOME, r, "dom", home_all.at[r, my_dom])

        @pl.when(r + 1 < rounds)
        def _():
            count_pairs(r + 1, 0, chips)

        @pl.when(r == 0)
        def _():
            gathered(FULL, 0, "dom", full_all.at[my_dom])
            gathered(STATE, 0, "dom", state_all.at[my_dom])

        gathered(HOME, r, "dom", home_all.at[r, my_dom])

        @pl.loop(0, n_dom)
        def _(p):
            grads = home_all[r, 0].astype(f32)
            for d in range(1, n_dom):
                grads = jnp.where(plan[r, d] == p, home_all[r, d].astype(f32), grads)
            state = state_all[p] + jnp.sum(grads * grads, axis=0, keepdims=True) / width
            state_all[p] = state
            full_all[p] = full_all[p] - (LEARN * grads) / jnp.sqrt(state)

        @pl.when(r + 1 < rounds)
        def _():
            src_all[r + 1, :, span(my_grp, src_dev)] = full_all[plan[r + 1, my_dom]].astype(bf16)

    src[...] = full_all[my_dom]
    src_state[...] = state_all[my_dom]


def shards(
    n_dom,
    n_grp,
    src_table,
    src_state,
    tgt_table,
    tgt_state,
    pair_source,
    pair_owner,
    pair_offset,
    negatives,
    plan,
):
    rounds, pairs = pair_source.shape
    src_dev, width = src_table.shape
    tgt_dev = tgt_table.shape[0]
    src_part = n_grp * src_dev
    chips = n_grp // 2
    f32, bf16 = jnp.float32, jnp.bfloat16
    vmem = pl.BlockSpec(memory_space=pltpu.VMEM)
    steps = max(n_dom, n_grp)
    new_src, new_src_state, new_tgt, new_tgt_state = pl.pallas_call(
        functools.partial(train_kernel, n_dom, n_grp, rounds),
        out_shape=(
            jax.ShapeDtypeStruct((width, src_dev), f32),
            jax.ShapeDtypeStruct((1, src_dev), f32),
            jax.ShapeDtypeStruct((width, tgt_dev), f32),
            jax.ShapeDtypeStruct((1, tgt_dev), f32),
        ),
        in_specs=[pl.BlockSpec(memory_space=pltpu.SMEM)] + [vmem] * 8,
        out_specs=[vmem] * 4,
        scratch_shapes=[
            pltpu.VMEM((n_grp, 2, rounds, pairs), jnp.int32),
            pltpu.VMEM((tgt_dev, 1), f32),
            pltpu.VMEM((width, tgt_dev), bf16),
            pltpu.VMEM((tgt_dev, width), bf16),
            pltpu.VMEM((n_dom, width, src_dev), bf16),
            pltpu.VMEM((n_dom, width, src_dev), f32),
            pltpu.VMEM((n_dom, 1, src_dev), f32),
            pltpu.VMEM((rounds, width, src_part), bf16),
            pltpu.VMEM((tgt_dev, src_part), f32),
            pltpu.VMEM((tgt_dev, src_part), f32),
            pltpu.VMEM((tgt_dev, src_part), bf16),
            pltpu.VMEM((tgt_dev, src_part), bf16),
            pltpu.VMEM((rounds, n_grp, 2, src_part), f32),
            pltpu.VMEM((rounds, n_grp, 1, src_part), f32),
            pltpu.VMEM((rounds, chips, width, 2 * src_dev), bf16),
            pltpu.VMEM((rounds, chips, width, src_dev), bf16),
            pltpu.VMEM((rounds, chips, width, src_dev), bf16),
            pltpu.VMEM((rounds, chips, width, src_dev), bf16),
            pltpu.VMEM((rounds, n_dom, width, src_dev), bf16),
            pltpu.SemaphoreType.DMA((rounds, KINDS, steps)),
            pltpu.SemaphoreType.DMA((rounds, KINDS, steps)),
        ],
        compiler_params=pltpu.CompilerParams(
            collective_id=0, has_side_effects=True, vmem_limit_bytes=56 * 1024 * 1024
        ),
        name="train",
    )(
        plan,
        negatives,
        pair_source,
        pair_owner[:, :, 0],
        pair_offset,
        src_table.T,
        src_state[None, :],
        tgt_table.T,
        tgt_state[None, :],
    )
    return (new_src.T, new_src_state[0], new_tgt.T, new_tgt_state[0])


def solution(mesh):
    return jax.shard_map(
        functools.partial(shards, mesh.shape["dom"], mesh.shape["grp"]),
        mesh=mesh,
        in_specs=(
            P(("dom", "grp"), None),
            P(("dom", "grp")),
            P(("dom", "grp"), None),
            P(("dom", "grp")),
            P(None, ("dom", "grp")),
            P(None, ("dom", "grp"), None),
            P(None, ("dom", "grp")),
            P("dom", None),
            P(),
        ),
        out_specs=(
            P(("dom", "grp"), None),
            P(("dom", "grp")),
            P(("dom", "grp"), None),
            P(("dom", "grp")),
        ),
        check_vma=False,
    )
```

time: 157 us -> 108 us (0.69)
  Pallas kernels: 138 us -> 99.4 us
  local copies, waits for them, and re-layouts: 12.9 us -> 7.48 us
  other arithmetic: 4.64 us -> 0 us
    pallas_call x1, Pallas kernels: 138 us -> 99.4 us  [shards(): pl.pallas_call(functools.partial(train_kernel, n_dom, n_grp, rounds), out...]
    pallas_call x2 -> x0, other arithmetic: 3.31 us -> none  [shards(): pl.pallas_call(functools.partial(train_kernel, n_dom, n_grp, rounds), out...]
    broadcast_in_dim x2 -> x0, local copies, waits for them, and re-layouts: 3.09 us -> none  [the longest x1 1.71 us: shards(): tgt_state[:, None]]
    unnamed x4 -> x7, local copies, waits for them, and re-layouts: 9.14 us -> 7.48 us
where the time goes in v2:
time: 108 us
  Pallas kernels  99.4 us (92%)
  local copies, waits for them, and re-layouts  7.48 us (7%)
    pallas_call x1, Pallas kernels, shards(): pl.pallas_call(functools.partial(train_kernel, n_dom, n_grp, rounds), out...  99.4 us
    unnamed x7, local copies, waits for them, and re-layouts  7.48 us

profile of v2, /device:TPU:0, one launch (start us, length us, event | category | flops | bytes accessed | tf_op | source)
XLA Modules:
  0.0 107.5 jit_solution(1936964327343296861)
XLA Ops:
  0.6 1.3 %copy.15 = s32[2,1024,1]{1,0,2:T(2,128)} copy(s32[2,1024,1]{1,2,0:T(1,128)} %param.14) | data formatting | bytes 16384
  1.9 99.4 %train.1 = (f32[400,128]{1,0:T(8,128)}, f32[1,128]{1,0:T(1,128)}, f32[400,1024]{1,0:T(8,128)}, f32[1,1024]{1,0:T(1,128)}) custom-call(s32[2,4]{1,0:T(2,128)} %plan.1, s32[1,1000]{1,0:T(1,128)} %negs.1, s32[2,1024]{1,0:T(2,128)} %pair_source.1, s32[2,1024]{1,0:T(2,128)} %bitcast.15, s32[2,1024]{1,0:T(2,128)} %pair_offset.1, f32[400,128]{1,0:T(8,128)} %bitcast.14, ...), custom_call_target="tpu_custom_call" | custom-call | tf_op jit(solution)/shard_map/train/pallas_call | solution.py:342
  101.3 1.6 %copy.20 = f32[128,400]{0,1:T(8,128)} copy(f32[128,400]{0,1:T(8,128)} %bitcast.13) | data formatting | bytes 409600
  102.9 1.2 %copy.21 = f32[128]{0:T(128)} copy(f32[128]{0:T(128)} %bitcast.19) | data formatting | bytes 1024
  104.1 0.0 copy-start
  104.1 2.8 %copy.22 = f32[1024,400]{0,1:T(8,128)} copy(f32[1024,400]{0,1:T(8,128)} %bitcast.11) | data formatting | bytes 3276800
  106.9 0.0 copy-done
  106.9 0.6 copy.23
Async XLA Ops:
  104.1 2.8 %copy-start = (f32[1,1024]{1,0:T(1,128)S(1)}, f32[1,1024]{1,0:T(1,128)}, u32[]{:S(2)}) copy-start(f32[1,1024]{1,0:T(1,128)} %get-tuple-element.11) | copy-start | bytes 12292

commit v3 on v2

--- a/solution.py
+++ b/solution.py
@@ -39,9 +39,12 @@
     state_all,
     src_all,
     scores,
+    exps,
     pulls,
     counts,
-    weights,
+    exp_grads,
+    pull_grads,
+    scaled,
     stat_all,
     sum_all,
     part_own,
@@ -129,7 +132,8 @@
     full_all[my_dom] = src_in[...]
     state_all[my_dom] = src_state_in[...]
     name_all[my_grp, 0] = pair_source[...]
-    name_all[my_grp, 1] = pair_owner[...] * tgt_dev + pair_offset[...]
+    for r in range(rounds):
+        name_all[my_grp, 1, r : r + 1] = pair_owner[r] * tgt_dev + pair_offset[r : r + 1]
     pl.semaphore_wait(barrier, n_dom + n_grp - 2)
     spread(ROWS, 0, "dom", row_all.at[my_dom])
     spread(NAMES, 0, "grp", name_all.at[my_grp])
@@ -190,7 +194,9 @@
             def add_exp(i, total):
                 many = mult[rows_of(i)]
                 named = jnp.where(many > 0, scores[rows_of(i), columns], LOW)
-                return total + jnp.sum(many * jnp.exp(named - top), axis=0, keepdims=True)
+                grown = many * jnp.exp(named - top)
+                exps[rows_of(i), columns] = grown.astype(bf16)
+                return total + jnp.sum(grown, axis=0, keepdims=True)
 
             total = lax.fori_loop(0, tiles, add_exp, jnp.zeros((1, both), f32))
             stat_all[r, my_grp, 0:1, columns] = top
@@ -204,6 +210,14 @@
             score_chip(lax.rem(my_chip - (step - 1) + chips, chips))
 
         spread(STATS, r, "grp", stat_all.at[r, my_grp])
+
+        @pl.loop(0, chips)
+        def _(chip):
+            columns = span(chip, both)
+            exp_grads[:, columns] = jnp.dot(
+                tgt_bf[...], exps[:, columns], preferred_element_type=f32
+            )
+
         gathered(STATS, r, "grp", stat_all.at[r, my_grp])
         top = stat_all[r, 0, 0:1, :]
         for g in range(1, n_grp):
@@ -212,35 +226,32 @@
         for g in range(n_grp):
             total += stat_all[r, g, 1:2, :] * jnp.exp(stat_all[r, g, 0:1, :] - top)
         log_total = jnp.log(total)
-        part = 1.0 / total
+        part = jnp.exp(stat_all[r, my_grp, 0:1, :] - top) / total
 
         def pull(i, pulled):
-            found = scores[rows_of(i)]
-            gap = (top - found) + log_total
-            small = jnp.exp(-jnp.abs(gap))
-            miss = jnp.where(gap >= 0, 1.0, small) / (1.0 + small)
+            gap = (scores[rows_of(i)] - top) - log_total
+            miss = pl.reciprocal(1.0 + jnp.exp(jnp.minimum(gap, 80.0)), approx=True)
             miss = miss * counts[rows_of(i)].astype(f32)
-            pulls[rows_of(i)] = miss
+            pulls[rows_of(i)] = miss.astype(bf16)
             return pulled + jnp.sum(miss, axis=0, keepdims=True)
 
         pulled = lax.fori_loop(0, tiles, pull, jnp.zeros((1, src_part), f32))
         sum_all[r, my_grp] = pulled
         spread(SUMS, r, "grp", sum_all.at[r, my_grp])
 
-        @pl.loop(0, tiles)
-        def _(i):
-            many = mult[rows_of(i)]
-            named = jnp.where(many > 0, scores[rows_of(i)], LOW)
-            scores[rows_of(i)] = many * jnp.exp(named - top) * part
+        @pl.loop(0, chips)
+        def _(chip):
+            columns = span(chip, both)
+            pull_grads[:, columns] = jnp.dot(
+                tgt_bf[...], pulls[:, columns], preferred_element_type=f32
+            )
 
         gathered(SUMS, r, "grp", sum_all.at[r, my_grp])
         pulled = sum_all[r, 0]
         for g in range(1, n_grp):
             pulled += sum_all[r, g]
-
-        @pl.loop(0, tiles)
-        def _(i):
-            weights[rows_of(i)] = (pulled * scores[rows_of(i)] - pulls[rows_of(i)]).astype(bf16)
+        sum_all[r, my_grp] = pulled * part
+        factor = sum_all.at[r, my_grp]
 
         mine, other = span(my_core, src_dev), span(1 - my_core, src_dev)
 
@@ -260,19 +271,21 @@
         for turn in range(1, chips + 1):
             step = turn % chips
             columns = span(lax.rem(my_chip + step, chips), both)
-            part_own[r, step] = jnp.dot(
-                tgt_bf[...], weights[:, columns], preferred_element_type=f32
+            part_own[r, step] = (
+                exp_grads[:, columns] * factor[:, columns] - pull_grads[:, columns]
             ).astype(bf16)
             give_part(step).start()
             if turn > 1:
                 back_out[r, turn - 1] = chip_sum(turn - 1).astype(bf16)
                 give_back(turn - 1).start()
 
+        scaled[...] = (src_all[r].astype(f32) * factor[...]).astype(bf16)
+
         @pl.loop(0, tiles)
         def _(i):
             grads = lax.dot_general(
-                src_all[r], weights[rows_of(i)], NT, preferred_element_type=f32
-            )
+                scaled[...], exps[rows_of(i)], NT, preferred_element_type=f32
+            ) - lax.dot_general(src_all[r], pulls[rows_of(i)], NT, preferred_element_type=f32)
             state = tgt_state[:, rows_of(i)] + jnp.sum(grads * grads, axis=0, keepdims=True) / width
             tgt_state[:, rows_of(i)] = state
             rows = tgt[:, rows_of(i)] - (LEARN * grads) / jnp.sqrt(state)
@@ -316,6 +329,18 @@
 
     src[...] = full_all[my_dom]
     src_state[...] = state_all[my_dom]
+
+
+def hand_out(*refs):
+    sources, targets, sems = refs[:4], refs[4:8], refs[8]
+    copies = [
+        pltpu.make_async_copy(source, target, sems.at[i])
+        for i, (source, target) in enumerate(zip(sources, targets))
+    ]
+    for each in copies:
+        each.start()
+    for each in copies:
+        each.wait()
 
 
 def shards(
@@ -339,7 +364,7 @@
     f32, bf16 = jnp.float32, jnp.bfloat16
     vmem = pl.BlockSpec(memory_space=pltpu.VMEM)
     steps = max(n_dom, n_grp)
-    new_src, new_src_state, new_tgt, new_tgt_state = pl.pallas_call(
+    trained = pl.pallas_call(
         functools.partial(train_kernel, n_dom, n_grp, rounds),
         out_shape=(
             jax.ShapeDtypeStruct((width, src_dev), f32),
@@ -359,9 +384,12 @@
             pltpu.VMEM((n_dom, 1, src_dev), f32),
             pltpu.VMEM((rounds, width, src_part), bf16),
             pltpu.VMEM((tgt_dev, src_part), f32),
-            pltpu.VMEM((tgt_dev, src_part), f32),
             pltpu.VMEM((tgt_dev, src_part), bf16),
             pltpu.VMEM((tgt_dev, src_part), bf16),
+            pltpu.VMEM((tgt_dev, src_part), bf16),
+            pltpu.VMEM((width, src_part), f32),
+            pltpu.VMEM((width, src_part), f32),
+            pltpu.VMEM((width, src_part), bf16),
             pltpu.VMEM((rounds, n_grp, 2, src_part), f32),
             pltpu.VMEM((rounds, n_grp, 1, src_part), f32),
             pltpu.VMEM((rounds, chips, width, 2 * src_dev), bf16),
@@ -380,13 +408,22 @@
         plan,
         negatives,
         pair_source,
-        pair_owner[:, :, 0],
+        pair_owner.transpose(0, 2, 1),
         pair_offset,
         src_table.T,
         src_state[None, :],
         tgt_table.T,
         tgt_state[None, :],
     )
+    anywhere = pl.BlockSpec(memory_space=pl.ANY)
+    new_src, new_src_state, new_tgt, new_tgt_state = pl.pallas_call(
+        hand_out,
+        out_shape=[jax.ShapeDtypeStruct(x.shape, x.dtype) for x in trained],
+        in_specs=[anywhere] * 4,
+        out_specs=[anywhere] * 4,
+        scratch_shapes=[pltpu.SemaphoreType.DMA((4,))],
+        name="hand_out",
+    )(*trained)
     return (new_src.T, new_src_state[0], new_tgt.T, new_tgt_state[0])
 
 

time: 108 us -> 154 us (1.43)
  Pallas kernels: 99.4 us -> 153 us
  local copies, waits for them, and re-layouts: 7.48 us -> 0 us
    pallas_call x0 -> x1, Pallas kernels: none -> 57.1 us  [shards(): pl.pallas_call(hand_out, out_shape=[jax.ShapeDtypeStruct(x.shape, x.dtype...]
    unnamed x7 -> x0, local copies, waits for them, and re-layouts: 7.48 us -> none
    pallas_call x1, Pallas kernels: 99.4 us -> 96.3 us  [shards(): pl.pallas_call(functools.partial(train_kernel, n_dom, n_grp, rounds), out...]
where the time goes in v3:
time: 154 us
  Pallas kernels  153 us (99%)
    pallas_call x1, Pallas kernels, shards(): pl.pallas_call(functools.partial(train_kernel, n_dom, n_grp, rounds), out...  96.3 us
    pallas_call x1, Pallas kernels, shards(): pl.pallas_call(hand_out, out_shape=[jax.ShapeDtypeStruct(x.shape, x.dtype...  57.1 us

profile of v3, /device:TPU:0, one launch (start us, length us, event | category | flops | bytes accessed | tf_op | source)
XLA Modules:
  0.0 154.0 jit_solution(8895829366715873839)
XLA Ops:
  0.6 96.3 %train.1 = (f32[400,128]{1,0:T(8,128)}, f32[1,128]{1,0:T(1,128)}, f32[400,1024]{1,0:T(8,128)}, f32[1,1024]{1,0:T(1,128)}) custom-call(s32[2,4]{1,0:T(2,128)} %plan.1, s32[1,1000]{1,0:T(1,128)} %negs.1, s32[2,1024]{1,0:T(2,128)} %pair_source.1, s32[2,1,1024]{2,1,0:T(1,128)} %bitcast.11, s32[2,1024]{1,0:T(2,128)} %pair_offset.1, f32[400,128]{1,0:T(8,128)} %bitcast.10, ...), custom_call_target="tpu_custom_call" | custom-call | tf_op jit(solution)/shard_map/train/pallas_call | solution.py:367
  96.9 57.1 %hand_out.1 = (f32[400,128]{1,0:T(8,128)}, f32[1,128]{1,0:T(1,128)}, f32[400,1024]{1,0:T(8,128)}, f32[1,1024]{1,0:T(1,128)}) custom-call(f32[400,128]{1,0:T(8,128)} %get-tuple-element.12.refs_0_, f32[1,128]{1,0:T(1,128)} %get-tuple-element.13.refs_1_, f32[400,1024]{1,0:T(8,128)} %get-tuple-element.14.refs_2_, f32[1,1024]{1,0:T(1,128)} %get-tuple-element.15.refs_3_), custom_call_target="tpu_custom_call" | custom-call | tf_op jit(solution)/shard_map/hand_out/pallas_call | solution.py:419

commit v4 on v3

--- a/solution.py
+++ b/solution.py
@@ -9,7 +9,7 @@
 
 LEARN = 0.1
 LOW = -1e30
-ROWS, STATS, SUMS, BACK, HOME, NAMES, GROUP, PASS, PART, FULL, STATE, KINDS = range(12)
+ROWS, STATS, SUMS, BACK, HOME, NAMES, GROUP, PASS, PART, FULL, STATE, BACK_LATE, HOME_LATE, KINDS = range(14)
 NT = (((1,), (1,)), ((), ()))
 
 
@@ -176,7 +176,7 @@
             spread(FULL, 0, "dom", full_all.at[my_dom])
             spread(STATE, 0, "dom", state_all.at[my_dom])
 
-        count_pairs(r, chips, n_grp)
+            count_pairs(0, chips, n_grp)
 
         def score_chip(chip):
             columns = span(chip, both)
@@ -260,9 +260,15 @@
                 PART, r, "grp", step, sibling, part_own.at[r, step, :, other], part_got.at[r, step]
             )
 
-        def give_back(step):
+        cut = width // 32 * 16
+        halves = ((BACK, HOME, pl.ds(0, cut)), (BACK_LATE, HOME_LATE, pl.ds(cut, width - cut)))
+
+        def give_back(step, half):
             peer = lax.rem(my_chip + step, chips) * 2 + my_core
-            return copy(BACK, r, "grp", step, peer, back_out.at[r, step], back_all.at[r, step])
+            kind, _, rows = halves[half]
+            return copy(
+                kind, r, "grp", step, peer, back_out.at[r, step, rows], back_all.at[r, step, rows]
+            )
 
         def chip_sum(step):
             give_part(step).wait()
@@ -277,7 +283,24 @@
             give_part(step).start()
             if turn > 1:
                 back_out[r, turn - 1] = chip_sum(turn - 1).astype(bf16)
-                give_back(turn - 1).start()
+                give_back(turn - 1, 0).start()
+
+        for step in range(1, chips):
+            give_back(step, 1).start()
+
+        @pl.when(r + 1 < rounds)
+        def _():
+            count_pairs(r + 1, 0, chips)
+
+        give_part(0).wait()
+        for half in range(2):
+            _, kind, rows = halves[half]
+            grads = part_own[r, 0, rows, mine].astype(f32) + part_got[r, 0, rows].astype(f32)
+            for step in range(1, chips):
+                give_back(step, half).wait()
+                grads += back_all[r, step, rows].astype(f32)
+            home_all[r, my_dom, rows] = grads.astype(bf16)
+            spread(kind, r, "dom", home_all.at[r, my_dom, rows])
 
         scaled[...] = (src_all[r].astype(f32) * factor[...]).astype(bf16)
 
@@ -288,7 +311,7 @@
             ) - lax.dot_general(src_all[r], pulls[rows_of(i)], NT, preferred_element_type=f32)
             state = tgt_state[:, rows_of(i)] + jnp.sum(grads * grads, axis=0, keepdims=True) / width
             tgt_state[:, rows_of(i)] = state
-            rows = tgt[:, rows_of(i)] - (LEARN * grads) / jnp.sqrt(state)
+            rows = tgt[:, rows_of(i)] - grads * (LEARN / jnp.sqrt(state))
             tgt[:, rows_of(i)] = rows
 
             @pl.when(r + 1 < rounds)
@@ -296,23 +319,17 @@
                 tgt_bf[:, rows_of(i)] = rows.astype(bf16)
                 tgt_rows[rows_of(i)] = rows.T.astype(bf16)
 
-        grads = chip_sum(0)
-        for step in range(1, chips):
-            give_back(step).wait()
-            grads += back_all[r, step].astype(f32)
-        home_all[r, my_dom] = grads.astype(bf16)
-        spread(HOME, r, "dom", home_all.at[r, my_dom])
-
         @pl.when(r + 1 < rounds)
         def _():
-            count_pairs(r + 1, 0, chips)
+            count_pairs(r + 1, chips, n_grp)
 
         @pl.when(r == 0)
         def _():
             gathered(FULL, 0, "dom", full_all.at[my_dom])
             gathered(STATE, 0, "dom", state_all.at[my_dom])
 
-        gathered(HOME, r, "dom", home_all.at[r, my_dom])
+        for _, kind, rows in halves:
+            gathered(kind, r, "dom", home_all.at[r, my_dom, rows])
 
         @pl.loop(0, n_dom)
         def _(p):
@@ -321,7 +338,7 @@
                 grads = jnp.where(plan[r, d] == p, home_all[r, d].astype(f32), grads)
             state = state_all[p] + jnp.sum(grads * grads, axis=0, keepdims=True) / width
             state_all[p] = state
-            full_all[p] = full_all[p] - (LEARN * grads) / jnp.sqrt(state)
+            full_all[p] = full_all[p] - grads * (LEARN / jnp.sqrt(state))
 
         @pl.when(r + 1 < rounds)
         def _():
@@ -332,15 +349,8 @@
 
 
 def hand_out(*refs):
-    sources, targets, sems = refs[:4], refs[4:8], refs[8]
-    copies = [
-        pltpu.make_async_copy(source, target, sems.at[i])
-        for i, (source, target) in enumerate(zip(sources, targets))
-    ]
-    for each in copies:
-        each.start()
-    for each in copies:
-        each.wait()
+    for source, target in zip(refs[:4], refs[4:]):
+        target[...] = source[...]
 
 
 def shards(
@@ -415,13 +425,11 @@
         tgt_table.T,
         tgt_state[None, :],
     )
-    anywhere = pl.BlockSpec(memory_space=pl.ANY)
     new_src, new_src_state, new_tgt, new_tgt_state = pl.pallas_call(
         hand_out,
         out_shape=[jax.ShapeDtypeStruct(x.shape, x.dtype) for x in trained],
-        in_specs=[anywhere] * 4,
-        out_specs=[anywhere] * 4,
-        scratch_shapes=[pltpu.SemaphoreType.DMA((4,))],
+        in_specs=[vmem] * 4,
+        out_specs=[vmem] * 4,
         name="hand_out",
     )(*trained)
     return (new_src.T, new_src_state[0], new_tgt.T, new_tgt_state[0])

time: 154 us -> 99.7 us (0.65)
  Pallas kernels: 153 us -> 98.9 us
    pallas_call x1, Pallas kernels: 57.1 us -> 2.85 us  [shards(): pl.pallas_call(hand_out, out_shape=[jax.ShapeDtypeStruct(x.shape, x.dtype...]
where the time goes in v4:
time: 99.7 us; the launch traced here: 99.5 us
  Pallas kernels  98.9 us (99%)
    pallas_call x1, Pallas kernels, shards(): pl.pallas_call(functools.partial(train_kernel, n_dom, n_grp, rounds), out...  96 us
    pallas_call x1, Pallas kernels, shards(): pl.pallas_call(hand_out, out_shape=[jax.ShapeDtypeStruct(x.shape, x.dtype...  2.85 us

profile of v4, /device:TPU:0, one launch (start us, length us, event | category | flops | bytes accessed | tf_op | source)
XLA Modules:
  0.0 99.5 jit_solution(6936730195421666384)
XLA Ops:
  0.6 96.0 %train.1 = (f32[400,128]{1,0:T(8,128)}, f32[1,128]{1,0:T(1,128)}, f32[400,1024]{1,0:T(8,128)}, f32[1,1024]{1,0:T(1,128)}) custom-call(s32[2,4]{1,0:T(2,128)} %plan.1, s32[1,1000]{1,0:T(1,128)} %negs.1, s32[2,1024]{1,0:T(2,128)} %pair_source.1, s32[2,1,1024]{2,1,0:T(1,128)} %bitcast.11, s32[2,1024]{1,0:T(2,128)} %pair_offset.1, f32[400,128]{1,0:T(8,128)} %bitcast.10, ...), custom_call_target="tpu_custom_call" | custom-call | tf_op jit(solution)/shard_map/train/pallas_call | solution.py:377
  96.6 2.8 %hand_out.1 = (f32[400,128]{1,0:T(8,128)}, f32[1,128]{1,0:T(1,128)}, f32[400,1024]{1,0:T(8,128)}, f32[1,1024]{1,0:T(1,128)}) custom-call(f32[400,128]{1,0:T(8,128)} %get-tuple-element.12.refs_0_, f32[1,128]{1,0:T(1,128)} %get-tuple-element.13.refs_1_, f32[400,1024]{1,0:T(8,128)} %get-tuple-element.14.refs_2_, f32[1,1024]{1,0:T(1,128)} %get-tuple-element.15.refs_3_), custom_call_target="tpu_custom_call" | custom-call | tf_op jit(solution)/shard_map/hand_out/pallas_call | solution.py:428

commit v5 on v4

--- a/solution.py
+++ b/solution.py
@@ -107,7 +107,7 @@
                 lax.broadcasted_iota(jnp.int32, (src_dev, pairs), 0) == source, 1.0, 0.0
             ).astype(bf16)
 
-            @pl.loop(0, tiles)
+            @pl.loop(0, tiles, unroll=True)
             def _(i):
                 target_hot = jnp.where(
                     lax.broadcasted_iota(jnp.int32, (tile, pairs), 0) == target - i * tile, 1.0, 0.0
@@ -138,7 +138,7 @@
     spread(ROWS, 0, "dom", row_all.at[my_dom])
     spread(NAMES, 0, "grp", name_all.at[my_grp])
 
-    @pl.loop(0, tiles)
+    @pl.loop(0, tiles, unroll=True)
     def _(i):
         here = lax.broadcasted_iota(jnp.int32, (tile, negs.shape[1]), 0)
         wanted = negs[...] - (my_grp * tgt_dev + i * tile)
@@ -189,7 +189,7 @@
                 named = jnp.where(mult[rows_of(i)] > 0, found, LOW)
                 return jnp.maximum(top, jnp.max(named, axis=0, keepdims=True))
 
-            top = lax.fori_loop(0, tiles, score, jnp.full((1, both), LOW, f32))
+            top = lax.fori_loop(0, tiles, score, jnp.full((1, both), LOW, f32), unroll=True)
 
             def add_exp(i, total):
                 many = mult[rows_of(i)]
@@ -198,7 +198,7 @@
                 exps[rows_of(i), columns] = grown.astype(bf16)
                 return total + jnp.sum(grown, axis=0, keepdims=True)
 
-            total = lax.fori_loop(0, tiles, add_exp, jnp.zeros((1, both), f32))
+            total = lax.fori_loop(0, tiles, add_exp, jnp.zeros((1, both), f32), unroll=True)
             stat_all[r, my_grp, 0:1, columns] = top
             stat_all[r, my_grp, 1:2, columns] = total
 
@@ -211,7 +211,7 @@
 
         spread(STATS, r, "grp", stat_all.at[r, my_grp])
 
-        @pl.loop(0, chips)
+        @pl.loop(0, chips, unroll=True)
         def _(chip):
             columns = span(chip, both)
             exp_grads[:, columns] = jnp.dot(
@@ -235,11 +235,11 @@
             pulls[rows_of(i)] = miss.astype(bf16)
             return pulled + jnp.sum(miss, axis=0, keepdims=True)
 
-        pulled = lax.fori_loop(0, tiles, pull, jnp.zeros((1, src_part), f32))
+        pulled = lax.fori_loop(0, tiles, pull, jnp.zeros((1, src_part), f32), unroll=True)
         sum_all[r, my_grp] = pulled
         spread(SUMS, r, "grp", sum_all.at[r, my_grp])
 
-        @pl.loop(0, chips)
+        @pl.loop(0, chips, unroll=True)
         def _(chip):
             columns = span(chip, both)
             pull_grads[:, columns] = jnp.dot(
@@ -304,7 +304,7 @@
 
         scaled[...] = (src_all[r].astype(f32) * factor[...]).astype(bf16)
 
-        @pl.loop(0, tiles)
+        @pl.loop(0, tiles, unroll=True)
         def _(i):
             grads = lax.dot_general(
                 scaled[...], exps[rows_of(i)], NT, preferred_element_type=f32

time: 99.7 us -> 91.3 us (0.916)
  Pallas kernels: 98.9 us -> 90.5 us
    pallas_call x1, Pallas kernels: 96 us -> 87.6 us  [shards(): pl.pallas_call(functools.partial(train_kernel, n_dom, n_grp, rounds), out...]
where the time goes in v5:
time: 91.3 us; the launch traced here: 91.1 us
  Pallas kernels  90.5 us (99%)
    pallas_call x1, Pallas kernels, shards(): pl.pallas_call(functools.partial(train_kernel, n_dom, n_grp, rounds), out...  87.6 us
    pallas_call x1, Pallas kernels, shards(): pl.pallas_call(hand_out, out_shape=[jax.ShapeDtypeStruct(x.shape, x.dtype...  2.85 us

profile of v5, /device:TPU:0, one launch (start us, length us, event | category | flops | bytes accessed | tf_op | source)
XLA Modules:
  0.0 91.1 jit_solution(15995699481036358750)
XLA Ops:
  0.6 87.6 %train.1 = (f32[400,128]{1,0:T(8,128)}, f32[1,128]{1,0:T(1,128)}, f32[400,1024]{1,0:T(8,128)}, f32[1,1024]{1,0:T(1,128)}) custom-call(s32[2,4]{1,0:T(2,128)} %plan.1, s32[1,1000]{1,0:T(1,128)} %negs.1, s32[2,1024]{1,0:T(2,128)} %pair_source.1, s32[2,1,1024]{2,1,0:T(1,128)} %bitcast.11, s32[2,1024]{1,0:T(2,128)} %pair_offset.1, f32[400,128]{1,0:T(8,128)} %bitcast.10, ...), custom_call_target="tpu_custom_call" | custom-call | tf_op jit(solution)/shard_map/train/pallas_call | solution.py:377
  88.3 2.8 %hand_out.1 = (f32[400,128]{1,0:T(8,128)}, f32[1,128]{1,0:T(1,128)}, f32[400,1024]{1,0:T(8,128)}, f32[1,1024]{1,0:T(1,128)}) custom-call(f32[400,128]{1,0:T(8,128)} %get-tuple-element.12.refs_0_, f32[1,128]{1,0:T(1,128)} %get-tuple-element.13.refs_1_, f32[400,1024]{1,0:T(8,128)} %get-tuple-element.14.refs_2_, f32[1,1024]{1,0:T(1,128)} %get-tuple-element.15.refs_3_), custom_call_target="tpu_custom_call" | custom-call | tf_op jit(solution)/shard_map/hand_out/pallas_call | solution.py:428
